TPU v7x, 256 devices: a whole 4x4x8 slice. The times are simulated.
256 devices in a mesh: dp: 16 (over y, x), vocab: 16 (over z, core).
Axes of the slice: x: 4, y: 4, z: 8, core: 2. Of those that a mesh axis runs over, the one named last changes fastest.
Arguments:
- hidden_states: bfloat16 [4096, 1280], P('dp')
- head_weight: bfloat16 [1280, 77824], P('dp', 'vocab')
- teacher_logprobs: bfloat16 [4096, 77824], P('dp', 'vocab'), may hold values from -18 to -2
- teacher_dest: int32 [4096], P('dp'), may hold values from 0 to 4095, as said below
- lengths: int32 [32], P('dp'), may hold values from 21 to 128, as said below
Outputs:
- hidden_grad: float32 [4096, 1280], P('dp', 'vocab')
- token_loss: float32 [4096], P('dp')
Inputs may be any that keep to these rules, and one draw needn't show every extreme that they name: teacher_dest is a permutation of the 4096 rollout rows; the 256 teacher rows of each data group go to every data group in equal numbers, 16 to each. `lengths`: sample k covers rollout rows k * 128 to (k + 1) * 128 - 1.
All inputs are finite; a program needn't handle non-finite values.
Results may differ from a plain program's by a relative error of at most 0.004.
Values may be sent and summed in bfloat16 or wider, within the bound.
A program may use at most 128 MiB of HBM per device.

v0:
```python
import jax
import jax.numpy as jnp
from jax import lax
from jax.sharding import PartitionSpec as P

SLOT = 128


def per_device(hidden_states, head_weight, teacher_logprobs, teacher_dest, lengths):
    tok_rows = hidden_states.shape[0]
    groups = lax.axis_size("dp")
    share_rows = tok_rows // groups
    row_ids = jnp.arange(tok_rows, dtype=jnp.int32)
    dest_group = teacher_dest // tok_rows
    local_pos = teacher_dest % tok_rows
    member = (dest_group[:, None] == jnp.arange(groups, dtype=jnp.int32)[None, :]).astype(jnp.int32)
    ranking = jnp.sum((jnp.cumsum(member, axis=0) - 1) * member, axis=1)
    slot_index = dest_group * share_rows + ranking
    select = slot_index[None, :] == row_ids[:, None]
    sent_pos = jnp.sum(jnp.where(select, local_pos[None, :], 0), axis=1)
    arrived_pos = lax.all_to_all(sent_pos, "dp", split_axis=0, concat_axis=0, tiled=True)
    placing = arrived_pos[None, :] == row_ids[:, None]
    samples = lengths.shape[0]
    sample_len = jnp.sum(
        jnp.where(
            (row_ids // SLOT)[:, None] == jnp.arange(samples, dtype=jnp.int32)[None, :],
            lengths[None, :],
            0,
        ),
        axis=1,
    )
    valid_rows = (row_ids % SLOT < sample_len).astype(jnp.float32)
    token_count = lax.psum(jnp.sum(valid_rows), "dp")
    loss_scale = tok_rows * groups / token_count
    ordered = jnp.dot(
        select.astype(jnp.bfloat16), teacher_logprobs, preferred_element_type=jnp.float32
    ).astype(jnp.bfloat16)
    arrived = lax.all_to_all(ordered, "dp", split_axis=0, concat_axis=0, tiled=True)
    aligned = jnp.dot(
        placing.astype(jnp.bfloat16), arrived, preferred_element_type=jnp.float32
    ).astype(jnp.bfloat16)
    weight = valid_rows * loss_scale
    logits = jnp.dot(
        hidden_states,
        lax.all_gather(head_weight, "dp", axis=0, tiled=True),
        preferred_element_type=jnp.float32,
    )
    targets = aligned.astype(jnp.float32)
    row_max = lax.pmax(jnp.max(logits, axis=1), "vocab")
    exponent = jnp.exp(logits - row_max[:, None])
    row_total, moment = lax.psum(
        (jnp.sum(exponent, axis=1), jnp.sum(exponent * (logits - targets), axis=1)), "vocab"
    )
    mean_gap = moment / row_total
    token_loss = weight * (mean_gap - row_max - jnp.log(row_total))
    logit_grad = (
        weight[:, None] * exponent / row_total[:, None] * (logits - targets - mean_gap[:, None])
    ).astype(jnp.bfloat16)
    partial_grad = lax.dot_general(
        logit_grad,
        lax.all_gather(head_weight, "dp", axis=0, tiled=True),
        (((1,), (1,)), ((), ())),
        preferred_element_type=jnp.float32,
    )
    hidden_grad = lax.psum_scatter(partial_grad, "vocab", scatter_dimension=1, tiled=True)
    return (hidden_grad, token_loss)


def solution(mesh):
    placed = (P("dp", None), P("dp", "vocab"), P("dp", "vocab"), P("dp"), P("dp"))
    return jax.shard_map(
        per_device,
        mesh=mesh,
        in_specs=placed,
        out_specs=(P("dp", "vocab"), P("dp")),
        check_vma=False,
    )
```

profile of v0, /device:TPU:24, one launch (start us, length us, event | category | flops | bytes accessed | tf_op | source)
XLA Modules:
  0.0 275.0 jit_solution(8931309697058469899)
XLA Ops:
  7.2 0.7 all-gather.2.cloned.1.call-update
  7.9 0.7 and_select_fusion
  8.6 0.6 reduce-window.6
  9.2 0.2 slice_reduce_fusion
  9.5 0.1 fusion.11
  9.6 0.1 select_reduce_fusion
  9.7 0.7 all_to_all.14
  10.4 7.2 %all-to-all-start = ((s32[16,16,1]{1,2,0:T(1,128)}), s32[16,16,1]{1,2,0:T(1,128)S(1)}, u32[]{:S(2)}, u32[]{:S(2)}) async-start(s32[16,16,1]{1,2,0:T(1,128)} %bitcast.2), calls=%async_computation | async-start | bytes 16384 | tf_op jit(solution)/shard_map/all_to_all | solution.py:21
  17.6 2.3 convolution_convert_fusion.1
  19.9 3.2 %all-to-all-done = s32[16,16,1]{1,2,0:T(1,128)S(1)} async-done(((s32[16,16,1]{1,2,0:T(1,128)}), s32[16,16,1]{1,2,0:T(1,128)S(1)}, u32[]{:S(2)}, u32[]{:S(2)}) %all-to-all-start) | async-done | bytes 1056 | tf_op jit(solution)/shard_map/all_to_all | solution.py:21
  23.0 6.4 %all-to-all-start.1 = ((bf16[16,16,4864]{2,1,0:T(8,128)(2,1)}), bf16[16,16,4864]{2,1,0:T(8,128)(2,1)}, u32[]{:S(2)}, u32[]{:S(2)}) async-start(bf16[16,16,4864]{2,1,0:T(8,128)(2,1)} %bitcast.25), calls=%async_computation.1 | async-start | bytes 4980736 | tf_op jit(solution)/shard_map/all_to_all | solution.py:38
  29.5 0.1 fusion.13
  29.5 0.6 convert_reduce_fusion
  30.2 68.7 %psum.21 = f32[]{:T(128)} all-reduce(f32[]{:T(128)} %get-tuple-element.8), channel_id=1, replica_groups=mesh['dp'=16,'vocab'=16] {'dp'}, use_global_device_ids=true, to_apply=%region_2.3 | all-reduce | flops 1 | bytes 8 | tf_op jit(solution)/shard_map/psum | solution.py:33
  99.6 0.5 broadcast.119
  100.1 0.7 reduce.5
  100.9 33.1 %all-gather.2.cloned.1.call-done = bf16[1280,4864]{1,0:T(8,128)(2,1)} async-done(((bf16[80,4864]{1,0:T(8,128)(2,1)}), bf16[1280,4864]{1,0:T(8,128)(2,1)}) %all-gather.2.cloned.1.call-update) | async-done | bytes 12451856 | tf_op jit(solution)/shard_map/all_gather | solution.py:45
  134.0 9.8 %fusion.17 = (f32[256]{0:T(256)S(1)}, f32[256,4864]{1,0:T(8,128)}) fusion(bf16[256,1280]{1,0:T(8,128)(2,1)S(1)} %copy-done.2, bf16[1280,4864]{1,0:T(8,128)(2,1)} %all-gather.2.cloned.1.call-done), kind=kOutput, calls=%fused_computation.46 | convolution fusion | flops 3188915968 | bytes 18088960 | tf_op jit(solution)/shard_map/dot_general | solution.py:43
  143.7 26.4 %pmax.7 = f32[256]{0:T(256)S(1)} all-reduce(f32[256]{0:T(256)S(1)} %get-tuple-element.13), channel_id=1, replica_groups=mesh['dp'=16,'vocab'=16] {'vocab'}, use_global_device_ids=true, to_apply=%region_4.5 | all-reduce | flops 256 | bytes 2048 | tf_op jit(solution)/shard_map/pmax | solution.py:49
  170.1 6.9 %fusion.2 = (f32[256]{0:T(256)S(1)}, f32[256]{0:T(256)S(1)}, f32[256,4864]{1,0:T(8,128)}) fusion(f32[256,4864]{1,0:T(8,128)} %get-tuple-element.14, f32[256]{0:T(256)S(1)} %pmax.7, bf16[256,4864]{1,0:T(8,128)(2,1)} %bitcast.4, s32[256]{0:T(256)S(1)} %eq.80), kind=kOutput, calls=%fused_computation.7 | convolution fusion | flops 646315520 | bytes 12455936 | tf_op jit(solution)/shard_map/dot_general | solution.py:39
  177.0 23.5 %all-reduce = (f32[256]{0:T(256)S(1)}, f32[256]{0:T(256)S(1)}) all-reduce(f32[256]{0:T(256)S(1)} %get-tuple-element.3, f32[256]{0:T(256)S(1)} %get-tuple-element.2), channel_id=1, replica_groups=mesh['dp'=16,'vocab'=16] {'vocab'}, use_global_device_ids=true, to_apply=%region_12.13 | all-reduce | flops 512 | bytes 4096 | tf_op jit(solution)/shard_map/psum | solution.py:51
  200.5 0.6 subtract_multiply_fusion
  201.1 12.2 %fusion.3 = f32[256,1280]{0,1:T(8,128)} fusion(bf16[1280,4864]{1,0:T(8,128)(2,1)} %all-gather.2.cloned.1.call-done, f32[256,4864]{1,0:T(8,128)} %get-tuple-element.15, f32[256,4864]{1,0:T(8,128)} %get-tuple-element.14, f32[256]{0:T(256)S(1)} %get-tuple-element.7, f32[256]{0:T(256)S(1)} %get-tuple-element.5, f32[256]{0:T(256)S(1)} %pmax.7, ...), kind=kOutput, calls=%fused_computation.8 | convolution fusion | flops 3195142144 | bytes 23728128 | tf_op jit(solution)/shard_map/dot_general | solution.py:59
  213.3 54.9 %reduce-scatter.2.cloned.1.call-done = f32[256,80]{0,1:T(8,128)} async-done(((f32[256,1280]{0,1:T(8,128)}), f32[256,80]{0,1:T(8,128)}) %reduce-scatter.2.cloned.1.call-update) | async-done | bytes 81936 | tf_op jit(solution)/shard_map/reduce_scatter | solution.py:65
  (16 shorter events, 0.3 us)
Async XLA Ops:
  7.2 10.4 %copy-start = (bf16[256,4864]{1,0:T(8,128)(2,1)S(1)}, bf16[256,4864]{1,0:T(8,128)(2,1)}, u32[]{:S(2)}) copy-start(bf16[256,4864]{1,0:T(8,128)(2,1)} %param.7) | copy-start | bytes 7471108
  7.2 126.8 %all-gather.2.cloned.1.call-start = ((), (), s32[]{:S(2)}) async-start(), calls=%async_computation.3 | async-start | bytes 13230080 | tf_op jit(solution)/shard_map/all_gather | solution.py:45
  10.4 12.7 %all-to-all-start = ((s32[16,16,1]{1,2,0:T(1,128)}), s32[16,16,1]{1,2,0:T(1,128)S(1)}, u32[]{:S(2)}, u32[]{:S(2)}) async-start(s32[16,16,1]{1,2,0:T(1,128)} %bitcast.2), calls=%async_computation | async-start | bytes 16384 | tf_op jit(solution)/shard_map/all_to_all | solution.py:21
  17.5 11.9 %copy-start.1 = (s32[2]{0:T(128)S(1)}, s32[2]{0:T(128)}, u32[]{:S(2)}) copy-start(s32[2]{0:T(128)} %param.9) | copy-start | bytes 28
  17.6 116.4 %copy-start.2 = (bf16[256,1280]{1,0:T(8,128)(2,1)S(1)}, bf16[256,1280]{1,0:T(8,128)(2,1)}, u32[]{:S(2)}) copy-start(bf16[256,1280]{1,0:T(8,128)(2,1)} %param.5) | copy-start | bytes 1966084
  23.0 147.0 %all-to-all-start.1 = ((bf16[16,16,4864]{2,1,0:T(8,128)(2,1)}), bf16[16,16,4864]{2,1,0:T(8,128)(2,1)}, u32[]{:S(2)}, u32[]{:S(2)}) async-start(bf16[16,16,4864]{2,1,0:T(8,128)(2,1)} %bitcast.25), calls=%async_computation.1 | async-start | bytes 4980736 | tf_op jit(solution)/shard_map/all_to_all | solution.py:38
  29.4 238.7 %reduce-scatter.2.cloned.1.call-start = ((), (), s32[]{:S(2)}) async-start(), calls=%async_computation.4 | async-start | bytes 1392640 | tf_op jit(solution)/shard_map/reduce_scatter | solution.py:65
Sparse Core Ops, SparseCore 0:
  10.4 123.4 all-gather.1
  213.4 54.7 reduce-scatter.1
where the time goes:
time: 276 us; the launch traced here: 275 us
  blocking collectives  119 us (43%)
  waiting for transfers between devices  91.9 us (33%)
  matrix products  31.1 us (11%)
  between operations  14.8 us (5%)
  starting transfers between devices  13.6 us (5%)
  other arithmetic  3.51 us (1%)
    psum x1, blocking collectives, per_device(): token_count = lax.psum(jnp.sum(valid_rows), 'dp')  68.7 us
    reduce_scatter x1, waiting for transfers between devices, per_device(): lax.psum_scatter(partial_grad, 'vocab', scatter_dimension=1, tiled=True)  54.9 us
    all_gather x1, waiting for transfers between devices, per_device(): lax.all_gather(head_weight, 'dp', axis=0, tiled=True)  33.1 us
    pmax x1, blocking collectives, per_device(): row_max = lax.pmax(jnp.max(logits, axis=1), 'vocab')  26.4 us
    psum x1, blocking collectives, per_device(): lax.psum((jnp.sum(exponent, axis=1), jnp.sum(exponent * (logits - targets...  23.5 us
    dot_general x1, matrix products, per_device(): lax.dot_general(logit_grad, lax.all_gather(head_weight, 'dp', axis=0, til...  12.2 us
    dot_general x1, matrix products, per_device(): jnp.dot(hidden_states, lax.all_gather(head_weight, 'dp', axis=0, tiled=Tr...  9.77 us
    all_to_all x1, starting transfers between devices, per_device(): lax.all_to_all(sent_pos, 'dp', split_axis=0, concat_axis=0, tiled=True)  7.17 us
  transfers between devices with their start and end apart: 4, of which 3 were waited for; matrix products, arithmetic and copies ran while one was open for 6% of the time, Pallas kernels for 0%

commit v1 on v0

v1 whole, which is shorter than its diff:
```python
import functools

import jax
import jax.numpy as jnp
from jax import lax
from jax.experimental import pallas as pl
from jax.experimental.pallas import tpu as pltpu
from jax.sharding import PartitionSpec as P

MESH = pl.DeviceIdType.MESH
SLOT = 128
N_DP = 16
N_V = 16
N_Z = 8
TOK = 256
SHARE = 16
FEAT = 1280
FB = 80
VSH = 4864
CB = 1280
Q = 4
ROWS = 32
BIG = 1e30
F32, BF16 = jnp.float32, jnp.bfloat16


def col_start(x):
    return pl.multiple_of((19 * (x // 2) + 9 * (x % 2)) * 128, 128)


def kernel(dest_ref, len_ref, h_hbm, w_hbm, t_hbm, grad_ref, loss_ref,
           tin, hin, wbuf, tord, tbuf, hsend, hbuf, possend, posbuf, sel, sbuf,
           lbuf, gbuf, statcol, ycol, lossbuf, asend, arecv, bsend, brecv,
           part, corebuf, stm, stp, rm, rp, xs, xr, fs, fr,
           lsem, wx_s, wy_s, wf_s, w_r, pos_s, pos_r, hd_s, hd_r, hz_s, hz_r, hc_s, hc_r,
           t_s, t_r, a_s, a_r, b_s, b_r, c_s, c_r, m_s, m_r, p_s, p_r, x_s, x_r, f_s, f_r):
    dp = lax.axis_index("dp")
    v = lax.axis_index("vocab")
    x, y = dp % 4, dp // 4
    z, c = v // 2, v % 2

    def rcopy(src, dst, ss, rs, d, vv):
        return pltpu.make_async_remote_copy(
            src_ref=src, dst_ref=dst, send_sem=ss, recv_sem=rs, device_id=(d, vv), device_id_type=MESH)

    bar = pltpu.get_barrier_semaphore()

    def greet(d, vv):
        pl.semaphore_signal(bar, inc=1, device_id=(d, vv), device_id_type=MESH)

    for i in range(1, N_DP):
        greet((dp + i) % N_DP, v)
    for i in range(4):
        greet(y * 4 + (x + i) % 4, z * 2 + 1 - c)
    for i in range(1, N_Z):
        greet(dp, (z + i) % N_Z * 2 + c)
    pl.semaphore_wait(bar, 15 + 4 + 7)

    def w_x(i):
        xt = (x + i) % 4
        return rcopy(w_hbm.at[:, pl.ds(col_start(xt), CB)], wbuf.at[dp], wx_s.at[i], w_r.at[dp], y * 4 + xt, v)

    def y_to(i):
        return (y + i) % 4 * 4 + x

    def w_own_y(i):
        return rcopy(w_hbm.at[:, pl.ds(col_start(x), CB)], wbuf.at[dp], wy_s.at[0, i // 2], w_r.at[dp], y_to(i), v)

    def w_row_y(j, i):
        b = y * 4 + (x + j) % 4
        return rcopy(wbuf.at[b], wbuf.at[b], wy_s.at[j, i // 2], w_r.at[b], y_to(i), v)

    def w_fwd(j, i):
        b = (y + 4 - i) % 4 * 4 + (x + j) % 4
        return rcopy(wbuf.at[b], wbuf.at[b], wf_s.at[j], w_r.at[b], y_to(i), v)

    def w_arrived(b):
        rcopy(wbuf.at[b], wbuf.at[b], wx_s.at[0], w_r.at[b], dp, v).wait_recv()

    own_w = pltpu.make_async_copy(w_hbm.at[:, pl.ds(col_start(x), CB)], wbuf.at[dp], lsem.at[0])
    get_t = pltpu.make_async_copy(t_hbm, tin, lsem.at[1])
    get_h = pltpu.make_async_copy(h_hbm, hin, lsem.at[2])
    for i in (1, 3, 2):
        w_x(i).start()
    for i in (1, 3):
        w_own_y(i).start()
    own_w.start()
    get_t.start()
    get_h.start()

    drow = jnp.concatenate([dest_ref[0:1, :], dest_ref[1:2, :]], axis=1)
    grp = lax.shift_right_logical(drow, 8)
    pos = (drow & 255).astype(F32)
    member = (grp == lax.broadcasted_iota(jnp.int32, (N_DP, TOK), 0)).astype(BF16)
    upper = (lax.broadcasted_iota(jnp.int32, (TOK, TOK), 0)
             <= lax.broadcasted_iota(jnp.int32, (TOK, TOK), 1)).astype(BF16)
    rank = jnp.dot(member, upper, preferred_element_type=F32)
    slot = lax.broadcasted_iota(jnp.int32, (TOK, N_DP), 0)
    spread = (slot // SHARE == lax.broadcasted_iota(jnp.int32, (TOK, N_DP), 1)).astype(BF16)
    member_s = jnp.dot(spread, member, preferred_element_type=F32)
    rank_s = jnp.dot(spread, rank.astype(BF16), preferred_element_type=F32)
    want = (lax.broadcasted_iota(jnp.int32, (TOK, TOK), 0) % SHARE + 1).astype(F32)
    chosen = jnp.where((member_s > 0.5) & (rank_s == want), 1.0, 0.0)
    sel[...] = chosen.astype(BF16)
    sent = jnp.sum(chosen * pos, axis=1, keepdims=True)
    possend[:, 0:SHARE, :] = jnp.broadcast_to(sent, (TOK, 128)).reshape(N_DP, SHARE, 128)
    len0, len1 = jnp.minimum(len_ref[0], SLOT), jnp.minimum(len_ref[1], SLOT)
    possend[:, SHARE:SHARE + 8, :] = jnp.broadcast_to((len0 + len1).astype(F32), (N_DP, 8, 128))

    def pos_msg(i):
        d = (dp + i) % N_DP
        return rcopy(possend.at[d], posbuf.at[dp], pos_s.at[i], pos_r.at[dp], d, v)

    for i in range(1, N_DP):
        pos_msg(i).start()
    posbuf[pl.ds(dp, 1)] = possend[pl.ds(dp, 1)]

    get_t.wait()

    def order(j, _):
        cols = pl.ds(pl.multiple_of(j * 256, 256), 256)
        res = jnp.dot(sel[...], tin[:, cols], preferred_element_type=F32).astype(BF16)
        tord[:, :, :, cols] = res.reshape(Q, 4, SHARE, 256)
        return 0

    lax.fori_loop(0, VSH // 256, order, 0)

    def t_msg(q, i):
        xt = (x + i) % 4
        return rcopy(tord.at[q, :, :, pl.ds(col_start(xt), CB)], tbuf.at[q, :, x], t_s.at[q, i], t_r.at[q, x], y * 4 + xt, v)

    def t_own(q):
        return pltpu.make_async_copy(tord.at[q, :, :, pl.ds(col_start(x), CB)], tbuf.at[q, :, x], t_s.at[q, 0])

    for i in range(1, N_DP):
        s = (dp + N_DP - i) % N_DP
        rcopy(possend.at[s], posbuf.at[s], pos_s.at[0], pos_r.at[s], dp, v).wait_recv()
    pb = posbuf[:, 0:SHARE, :].reshape(TOK, 128)
    lane = lax.broadcasted_iota(jnp.int32, (TOK, 128), 1).astype(F32)
    sbuf[:, 0:128] = (pb == lane).astype(BF16)
    sbuf[:, 128:256] = (pb == lane + 128.0).astype(BF16)
    get_h.wait()
    for j in range(5):
        hsend[:, j * 256:(j + 1) * 256] = jnp.dot(
            sbuf[...], hin[:, j * 256:(j + 1) * 256], preferred_element_type=F32).astype(BF16)

    def h_msg(i):
        d = (dp + i) % N_DP
        return rcopy(hsend.at[pl.ds(pl.multiple_of(d // 4 * 64, 64), 64)], hbuf.at[v], hd_s.at[i], hd_r.at[0], d, v)

    @pl.when(dp == v)
    def _():
        for i in range(1, N_DP):
            h_msg(i).start()
        hbuf[pl.ds(v, 1)] = hsend[pl.ds(pl.multiple_of(y * 64, 64), 64)].reshape(1, 64, FEAT)

    for i in (1, 3, 2):
        t_msg(0, i).start()
    for q in range(Q):
        t_own(q).start()
    own_w.wait()

    for j in (1, 3, 2):
        w_arrived(y * 4 + (x + j) % 4)
        for i in (1, 3):
            w_row_y(j, i).start()
    for q in range(1, Q):
        for i in (1, 3, 2):
            t_msg(q, i).start()

    def h_z(b, i, k):
        return rcopy(hbuf.at[b], hbuf.at[b], hz_s.at[k], hz_r.at[b], dp, (z + i) % N_Z * 2 + c)

    def h_c(b, k):
        return rcopy(hbuf.at[b], hbuf.at[b], hc_s.at[k], hc_r.at[b], dp, z * 2 + 1 - c)

    def h_arrived(b):
        rcopy(hbuf.at[b], hbuf.at[b], hz_s.at[0], hz_r.at[b], dp, v).wait_recv()

    @pl.when(dp != v)
    def _():
        rcopy(hsend.at[pl.ds(0, 64)], hbuf.at[v], hd_s.at[0], hd_r.at[0], dp, v).wait_recv()

    h_z(v, 1, 0).start()
    h_z(v, N_Z - 1, 1).start()
    h_c(v, 0).start()

    def h_step(s):
        b = (v + N_V - 2 * s) % N_V
        h_arrived(b)
        if s < 4:
            h_z(b, 1, 2 * s).start()
        h_c(b, 2 * s - 1).start()
        if s < 4:
            b = (v + 2 * s) % N_V
            h_arrived(b)
            if s < 3:
                h_z(b, N_Z - 1, 2 * s + 1).start()
            h_c(b, 2 * s).start()

    def w_pass(j, i):
        w_arrived((y + 4 - i) % 4 * 4 + (x + j) % 4)
        w_fwd(j, i).start()

    w_pass(0, 1)
    h_step(1)
    w_pass(1, 1)
    w_pass(3, 3)
    h_step(2)
    w_pass(2, 3)
    h_step(3)
    h_step(4)
    for j in (2, 3):
        w_arrived((y + 3) % 4 * 4 + (x + j) % 4)
    for j in (0, 1):
        w_arrived((y + 1) % 4 * 4 + (x + j) % 4)
    for k in range(N_Z):
        b = k * 2 + 1 - c
        rcopy(hbuf.at[b], hbuf.at[b], hc_s.at[0], hc_r.at[b], dp, v).wait_recv()
    for j in range(4):
        w_arrived((y + 2) % 4 * 4 + (x + j) % 4)

    odd = x % 2
    lane_r = lax.broadcasted_iota(jnp.int32, (ROWS, 128), 1)
    me8 = x * 2 + c

    def a_msg(q, i):
        k = (me8 + i) % 8
        return rcopy(asend.at[q], arecv.at[q, me8], a_s.at[q, i], a_r.at[q, me8], y * 4 + k // 2, z * 2 + k % 2)

    def b_msg(q, i):
        return rcopy(bsend.at[q], brecv.at[q, z], b_s.at[q, i], b_r.at[q, z], dp, (z + i) % N_Z * 2 + c)

    def c_msg(q):
        return rcopy(part.at[q, :, 1 - c], corebuf.at[q], c_s.at[q], c_r.at[q], dp, z * 2 + 1 - c)

    def m_msg(q, s):
        return rcopy(stm.at[q, s], rm.at[q, s], m_s.at[q, s], m_r.at[q, s], dp, (z + N_Z - 1) % N_Z * 2 + c)

    def p_msg(q, s):
        return rcopy(stp.at[q, s], rp.at[q, s], p_s.at[q, s], p_r.at[q, s], dp, (z + 1) % N_Z * 2 + c)

    def x_msg(q, i):
        xt = (x + i) % 4
        return rcopy(xs.at[q, xt], xr.at[q, x], x_s.at[q, i], x_r.at[q, x], y * 4 + xt, v)

    def f_msg(q):
        return rcopy(fs.at[q], fr.at[y], f_s.at[q], f_r.at[y], q * 4 + x, v)

    def combine(got):
        halves = []
        for r in (0, 4):
            mxs = got[:, r:r + 1, :]
            mx = jnp.max(mxs, axis=0)
            scale = jnp.exp(mxs - mx[None])
            halves.append((mx, jnp.sum(scale * got[:, r + 1:r + 2, :], axis=0),
                           jnp.sum(scale * got[:, r + 2:r + 3, :], axis=0)))
        return halves

    def stage0(q):
        t_own(q).wait()
        for i in (1, 3, 2):
            s = (x + 4 - i) % 4
            rcopy(tord.at[q, :, :, pl.ds(0, CB)], tbuf.at[q, :, s], t_s.at[q, 0], t_r.at[q, s], dp, v).wait_recv()
        hq = hbuf[pl.ds(q * 4, 4)].reshape(TOK, FEAT)
        for j in range(5):
            wj = wbuf[:, :, j * 256:(j + 1) * 256].reshape(FEAT, 256)
            out = jnp.dot(hq, wj, preferred_element_type=F32)
            if j == 0:
                hidden = (lax.broadcasted_iota(jnp.int32, (TOK, 256), 1) < 128) & (odd == 1)
                out = jnp.where(hidden, -BIG, out)
            lbuf[q, :, j * 256:(j + 1) * 256] = out

        def rows(r, _):
            at = pl.ds(pl.multiple_of(r * ROWS, ROWS), ROWS)
            logits = lbuf[q, at, :]
            targets = tbuf[q, r // 2, pl.ds(r % 2 * 2, 2)].reshape(ROWS, CB).astype(F32)
            mx = jnp.max(logits, axis=1, keepdims=True)
            e = jnp.exp(logits - mx)
            tot = jnp.sum(e, axis=1, keepdims=True)
            mom = jnp.sum(e * (logits - targets), axis=1, keepdims=True)
            base = r // 4 * 4
            statcol[at, :] = jnp.where(lane_r == base, mx, jnp.where(
                lane_r == base + 1, tot, jnp.where(lane_r == base + 2, mom, 0.0)))
            return 0

        lax.fori_loop(0, TOK // ROWS, rows, 0)
        packed = (statcol[0:128, :] + statcol[128:256, :]).T[0:8, :]
        asend[q] = packed
        for i in range(1, 8):
            a_msg(q, i).start()
        arecv[q, pl.ds(me8, 1)] = packed[None]

    def stage1(q):
        for i in range(1, 8):
            s = (me8 + i) % 8
            rcopy(asend.at[q], arecv.at[q, s], a_s.at[q, 0], a_r.at[q, s], dp, v).wait_recv()
        (m0, t0, o0), (m1, t1, o1) = combine(arecv[q])
        pad = jnp.zeros((1, 128), F32)
        packed = jnp.concatenate([m0, t0, o0, pad, m1, t1, o1, pad], axis=0)
        bsend[q] = packed
        for i in range(1, N_Z):
            b_msg(q, i).start()
        brecv[q, pl.ds(z, 1)] = packed[None]

    def stage2(q):
        for i in range(1, N_Z):
            s = (z + i) % N_Z
            rcopy(bsend.at[q], brecv.at[q, s], b_s.at[q, 0], b_r.at[q, s], dp, v).wait_recv()
        rows8 = []
        for mx, tot, mom in combine(brecv[q]):
            gap = mom / tot
            rows8 += [mx, 1.0 / tot, gap, gap - mx - jnp.log(tot)]
        cols = jnp.concatenate(rows8 + [jnp.zeros((120, 128), F32)], axis=0).T
        ycol[...] = cols
        lane_f = lax.broadcasted_iota(jnp.int32, (128, 128), 1)
        for half in range(2):
            lossbuf[q, half * 128:(half + 1) * 128, :] = jnp.where(
                lane_f == FB, cols[:, 4 * half + 3:4 * half + 4], 0.0)

            def rows(r, _, half=half):
                yat = pl.ds(pl.multiple_of(r * ROWS, ROWS), ROWS)
                at = pl.ds(pl.multiple_of(half * 128 + r * ROWS, ROWS), ROWS)
                rr = half * 4 + r
                yc = ycol[yat, :]
                mx, inv, gap = (yc[:, 4 * half + k:4 * half + k + 1] for k in range(3))
                logits = lbuf[q, at, :]
                targets = tbuf[q, rr // 2, pl.ds(rr % 2 * 2, 2)].reshape(ROWS, CB).astype(F32)
                gbuf[at, :] = (jnp.exp(logits - mx) * inv * (logits - targets - gap)).astype(BF16)
                return 0

            lax.fori_loop(0, 4, rows, 0)

        def grads(j, _):
            wj = wbuf[pl.ds(j * 4, 4)].reshape(4 * FB, CB)
            out = lax.dot_general(wj, gbuf[...], (((1,), (1,)), ((), ())), preferred_element_type=F32)
            part[q, pl.ds(j * 2, 2)] = out.reshape(2, 2, FB, TOK)
            return 0

        lax.fori_loop(0, 4, grads, 0)
        c_msg(q).start()

    def own(q, dz):
        d = (z + dz) % N_Z
        return part[q, d, c] + corebuf[q, d]

    def stage3(q):
        c_msg(q).wait_recv()
        stm[q, 0] = own(q, 4).astype(BF16)
        m_msg(q, 0).start()
        stp[q, 0] = own(q, 3).astype(BF16)
        p_msg(q, 0).start()

    def ring(q, s):
        m_msg(q, s - 1).wait_recv()
        stm[q, s] = (rm[q, s - 1].astype(F32) + own(q, 4 + s)).astype(BF16)
        m_msg(q, s).start()
        if s < 3:
            p_msg(q, s - 1).wait_recv()
            stp[q, s] = (rp[q, s - 1].astype(F32) + own(q, 3 - s)).astype(BF16)
            p_msg(q, s).start()

    def stage7(q):
        p_msg(q, 2).wait_recv()
        m_msg(q, 3).wait_recv()
        total = own(q, 0) + rp[q, 2].astype(F32) + rm[q, 3].astype(F32)
        padded = jnp.concatenate([total, jnp.zeros((128 - FB, TOK), F32)], axis=0)
        xs[q] = padded.T.reshape(4, 64, 128)
        for i in (1, 3, 2):
            x_msg(q, i).start()

    def stage8(q):
        total = xs[q, x] + lossbuf[q, pl.ds(pl.multiple_of(x * 64, 64), 64), :]
        for i in (1, 3, 2):
            s = (x + i) % 4
            rcopy(xs.at[q, 0], xr.at[q, s], x_s.at[q, 0], x_r.at[q, s], dp, v).wait_recv()
            total += xr[q, s]
        fs[q] = total

        @pl.when(y == q)
        def _():
            fr[pl.ds(y, 1)] = total[None]

        @pl.when(y != q)
        def _():
            f_msg(q).start()

    stages = [stage0, stage1, stage2, stage3, lambda q: ring(q, 1), lambda q: ring(q, 2), lambda q: ring(q, 3),
              stage7, stage8]

    def tick(tau, _):
        for s in reversed(range(len(stages))):
            q = tau - s

            @pl.when((q >= 0) & (q < Q))
            def _(s=s, q=q):
                stages[s](q)
        return 0

    lax.fori_loop(0, Q + len(stages) - 1, tick, 0)

    for i in range(1, 4):
        s = (y + i) % 4
        rcopy(fs.at[0], fr.at[s], f_s.at[0], f_r.at[s], dp, v).wait_recv()
    rows = fr[...].reshape(TOK, 128)
    hi = rows.astype(BF16)
    rest = rows - hi.astype(F32)
    mid = rest.astype(BF16)
    low = (rest - mid.astype(F32)).astype(BF16)
    placed = jnp.zeros((TOK, 128), F32)
    for piece in (low, mid, hi):
        placed += lax.dot_general(sbuf[...], piece, (((0,), (0,)), ((), ())), preferred_element_type=F32)
    count = jnp.sum(posbuf[:, SHARE:SHARE + 8, :], axis=0)[0:1, :]
    scale = float(TOK * N_DP) / count
    row = lax.broadcasted_iota(jnp.int32, (TOK, 128), 0)
    limit = jnp.where(row < SLOT, len0, len1)
    placed = jnp.where(row % SLOT < limit, placed * scale, 0.0)
    grad_ref[...] = placed[:, 0:FB]
    loss_ref[...] = placed.T[FB:FB + 1, :]

    for i in range(1, 4):
        w_x(i).wait_send()
    for i in (1, 3):
        w_own_y(i).wait_send()
        for j in range(1, 4):
            w_row_y(j, i).wait_send()
    for j, i in ((0, 1), (1, 1), (3, 3), (2, 3)):
        w_fwd(j, i).wait_send()
    for i in range(1, N_DP):
        pos_msg(i).wait_send()

    @pl.when(dp == v)
    def _():
        for i in range(1, N_DP):
            h_msg(i).wait_send()

    for k in range(7):
        h_z(v, 1, k).wait_send()
    for k in range(8):
        h_c(v, k).wait_send()

    def drain(q, _):
        for i in range(1, 4):
            t_msg(q, i).wait_send()
            x_msg(q, i).wait_send()
        for i in range(1, 8):
            a_msg(q, i).wait_send()
            b_msg(q, i).wait_send()
        c_msg(q).wait_send()
        for s in range(4):
            m_msg(q, s).wait_send()
        for s in range(3):
            p_msg(q, s).wait_send()

        @pl.when(y != q)
        def _():
            f_msg(q).wait_send()
        return 0

    lax.fori_loop(0, Q, drain, 0)


def per_device(hidden_states, head_weight, teacher_logprobs, teacher_dest, lengths):
    vm = pltpu.VMEM
    dma = pltpu.SemaphoreType.DMA
    grad, loss = pl.pallas_call(
        kernel,
        out_shape=(jax.ShapeDtypeStruct((TOK, FB), F32), jax.ShapeDtypeStruct((1, TOK), F32)),
        in_specs=[pl.BlockSpec(memory_space=pltpu.VMEM), pl.BlockSpec(memory_space=pltpu.SMEM)]
        + [pl.BlockSpec(memory_space=pl.ANY)] * 3,
        out_specs=(pl.BlockSpec(memory_space=pltpu.VMEM), pl.BlockSpec(memory_space=pltpu.VMEM)),
        scratch_shapes=[
            vm((TOK, VSH), BF16),
            vm((TOK, FEAT), BF16),
            vm((N_DP, FB, CB), BF16),
            vm((Q, 4, SHARE, VSH), BF16),
            vm((Q, 4, 4, SHARE, CB), BF16),
            vm((TOK, FEAT), BF16),
            vm((N_DP, 64, FEAT), BF16),
            vm((N_DP, SHARE + 8, 128), F32),
            vm((N_DP, SHARE + 8, 128), F32),
            vm((TOK, TOK), BF16),
            vm((TOK, TOK), BF16),
            vm((Q, TOK, CB), F32),
            vm((TOK, CB), BF16),
            vm((TOK, 128), F32),
            vm((128, 128), F32),
            vm((Q, TOK, 128), F32),
            vm((Q, 8, 128), F32),
            vm((Q, 8, 8, 128), F32),
            vm((Q, 8, 128), F32),
            vm((Q, N_Z, 8, 128), F32),
            vm((Q, N_Z, 2, FB, TOK), F32),
            vm((Q, N_Z, FB, TOK), F32),
            vm((Q, 4, FB, TOK), BF16),
            vm((Q, 3, FB, TOK), BF16),
            vm((Q, 4, FB, TOK), BF16),
            vm((Q, 3, FB, TOK), BF16),
            vm((Q, 4, 64, 128), F32),
            vm((Q, 4, 64, 128), F32),
            vm((Q, 64, 128), F32),
            vm((4, 64, 128), F32),
            dma((3,)),
            dma((4,)), dma((4, 2)), dma((4,)), dma((N_DP,)),
            dma((N_DP,)), dma((N_DP,)),
            dma((N_DP,)), dma((1,)),
            dma((8,)), dma((N_V,)),
            dma((8,)), dma((N_V,)),
            dma((Q, 4)), dma((Q, 4)),
            dma((Q, 8)), dma((Q, 8)),
            dma((Q, N_Z)), dma((Q, N_Z)),
            dma((Q,)), dma((Q,)),
            dma((Q, 4)), dma((Q, 4)),
            dma((Q, 3)), dma((Q, 3)),
            dma((Q, 4)), dma((Q, 4)),
            dma((Q,)), dma((4,)),
        ],
        compiler_params=pltpu.CompilerParams(
            collective_id=0, has_side_effects=True, vmem_limit_bytes=58 * 2**20),
        name="distill",
    )(teacher_dest.reshape(2, 128), lengths, hidden_states, head_weight, teacher_logprobs)
    return grad, loss.reshape(TOK)


def solution(mesh):
    placed = (P("dp", None), P("dp", "vocab"), P("dp", "vocab"), P("dp"), P("dp"))
    return jax.shard_map(
        per_device,
        mesh=mesh,
        in_specs=placed,
        out_specs=(P("dp", "vocab"), P("dp")),
        check_vma=False,
    )
```

time: 276 us -> 144 us (0.52)
  Pallas kernels: 0 us -> 140 us
  blocking collectives: 119 us -> 0 us
  waiting for transfers between devices: 91.9 us -> 0 us
  matrix products: 31.1 us -> 0 us
  between operations: 14.8 us -> 0.64 us
  starting transfers between devices: 13.6 us -> 0 us
  other arithmetic: 3.51 us -> 0 us
    pallas_call x0 -> x1, Pallas kernels: none -> 140 us  [per_device(): pl.pallas_call(kernel, out_shape=(jax.ShapeDtypeStruct((TOK, FB), F32), j...]
    psum x2 -> x0, blocking collectives: 92.3 us -> none  [the longest x1 68.7 us: per_device(): token_count = lax.psum(jnp.sum(valid_rows), 'dp')]
    reduce_scatter x1 -> x0, waiting for transfers between devices: 54.9 us -> none  [per_device(): lax.psum_scatter(partial_grad, 'vocab', scatter_dimension=1, tiled=True)]
    all_gather x1 -> x0, waiting for transfers between devices: 33.1 us -> none  [per_device(): lax.all_gather(head_weight, 'dp', axis=0, tiled=True)]
    dot_general x4 -> x0, matrix products: 31.1 us -> none  [the longest x1 12.2 us: per_device(): lax.dot_general(logit_grad, lax.all_gather(head_weight, 'dp', axis=0, til...]
    pmax x1 -> x0, blocking collectives: 26.4 us -> none  [per_device(): row_max = lax.pmax(jnp.max(logits, axis=1), 'vocab')]
    all_to_all x2 -> x0, starting transfers between devices: 13.5 us -> none  [the longest x1 7.17 us: per_device(): lax.all_to_all(sent_pos, 'dp', split_axis=0, concat_axis=0, tiled=True)]
    all_to_all x2 -> x0, waiting for transfers between devices: 3.19 us -> none  [the longest x1 3.18 us: per_device(): lax.all_to_all(sent_pos, 'dp', split_axis=0, concat_axis=0, tiled=True)]
  transfers between devices with their start and end apart: 4 -> 0, of which waited for: 3 -> 0; matrix products, arithmetic and copies ran while one was open for 6% -> 0% of each run, Pallas kernels for 0% -> 0%
where the time goes in v1:
time: 144 us
  Pallas kernels  140 us (97%)
  local copies, waits for them, and re-layouts  2.85 us (2%)
    pallas_call x1, Pallas kernels, per_device(): pl.pallas_call(kernel, out_shape=(jax.ShapeDtypeStruct((TOK, FB), F32), j...  140 us

profile of v1, /device:TPU:24, one launch (start us, length us, event | category | flops | bytes accessed | tf_op | source)
XLA Modules:
  0.0 143.7 jit_solution(1072023154378046549)
XLA Ops:
  0.6 140.2 %distill.1 = (f32[256,80]{1,0:T(8,128)}, f32[1,256]{1,0:T(1,128)}) custom-call(s32[2,128]{1,0:T(2,128)} %bitcast.2, s32[2]{0:T(128)} %len_ref.1, bf16[256,1280]{1,0:T(8,128)(2,1)} %h_hbm.1, bf16[80,4864]{1,0:T(8,128)(2,1)} %w_hbm.1, bf16[256,4864]{1,0:T(8,128)(2,1)} %t_hbm.1), custom_call_target="tpu_custom_call" | custom-call | tf_op jit(solution)/shard_map/distill/pallas_call | solution.py:466
  140.9 1.6 %copy.7 = f32[256,80]{0,1:T(8,128)} copy(f32[256,80]{1,0:T(8,128)} %get-tuple-element.6) | data formatting | bytes 163840
  142.5 1.2 copy.9

commit v2 on v1

v2 whole, which is shorter than its diff:
```python
import functools

import jax
import jax.numpy as jnp
from jax import lax
from jax.experimental import pallas as pl
from jax.experimental.pallas import tpu as pltpu
from jax.sharding import PartitionSpec as P

MESH = pl.DeviceIdType.MESH
SLOT = 128
N_DP = 16
N_V = 16
N_Z = 8
TOK = 256
SHARE = 16
FEAT = 1280
FB = 80
VSH = 4864
CB = 1280
CC, NC = 256, 5
Q = 4
ROWS = 32
BIG = 1e30
F32, BF16 = jnp.float32, jnp.bfloat16


def col_start(x):
    return pl.multiple_of((19 * (x // 2) + 9 * (x % 2)) * 128, 128)


def kernel(dest_ref, len_ref, h_hbm, w_hbm, t_hbm, out_ref, place_ref,
           tin, hin, wbuf, tord, tbuf, hsend, hbuf, possend, posbuf, sel, vbuf,
           lbuf, gbuf, statcol, ycol, lossbuf, asend, arecv, bsend, brecv,
           part, corebuf, xs, xr, zs, zr, tr, fs, fr,
           lsem, w_s, wx_r, wf_r, w_r, pos_s, pos_r, hd_s, hd_r, h_s, hz_r, hc_r,
           t_s, t_r, a_s, a_r, b_s, b_r, c_s, c_r, x_s, x_r, z_s, z_r, f_s, f_r):
    dp = lax.axis_index("dp")
    v = lax.axis_index("vocab")
    x, y = dp % 4, dp // 4
    z, c = v // 2, v % 2

    def rcopy(src, dst, ss, rs, d, vv):
        return pltpu.make_async_remote_copy(
            src_ref=src, dst_ref=dst, send_sem=ss, recv_sem=rs, device_id=(d, vv), device_id_type=MESH)

    bar = pltpu.get_barrier_semaphore()

    def greet(d, vv):
        pl.semaphore_signal(bar, inc=1, device_id=(d, vv), device_id_type=MESH)

    for i in range(1, N_DP):
        greet((dp + i) % N_DP, v)
    for i in range(4):
        greet(y * 4 + (x + i) % 4, z * 2 + 1 - c)
    for i in range(1, N_Z):
        greet(dp, (z + i) % N_Z * 2 + c)

    own_w = pltpu.make_async_copy(w_hbm.at[:, pl.ds(col_start(x), CB)], wbuf.at[dp], lsem.at[0])
    get_t = pltpu.make_async_copy(t_hbm, tin, lsem.at[1])
    get_h = pltpu.make_async_copy(h_hbm, hin, lsem.at[2])
    get_t.start()
    own_w.start()
    get_h.start()

    drow = jnp.concatenate([dest_ref[0:1, :], dest_ref[1:2, :]], axis=1)
    grp = lax.shift_right_logical(drow, 8)
    pos = (drow & 255).astype(F32)
    member = (grp == lax.broadcasted_iota(jnp.int32, (N_DP, TOK), 0)).astype(BF16)
    upper = (lax.broadcasted_iota(jnp.int32, (TOK, TOK), 0)
             <= lax.broadcasted_iota(jnp.int32, (TOK, TOK), 1)).astype(BF16)
    rank = jnp.dot(member, upper, preferred_element_type=F32)
    slot = lax.broadcasted_iota(jnp.int32, (TOK, N_DP), 0)
    spread = (slot // SHARE == lax.broadcasted_iota(jnp.int32, (TOK, N_DP), 1)).astype(BF16)
    member_s = jnp.dot(spread, member, preferred_element_type=F32)
    rank_s = jnp.dot(spread, rank.astype(BF16), preferred_element_type=F32)
    want = (lax.broadcasted_iota(jnp.int32, (TOK, TOK), 0) % SHARE + 1).astype(F32)
    chosen = jnp.where((member_s > 0.5) & (rank_s == want), 1.0, 0.0)
    sel[...] = chosen.astype(BF16)
    sent = jnp.sum(chosen * pos, axis=1, keepdims=True)
    lane0 = dp % 8 * SHARE
    lane_s = lax.broadcasted_iota(jnp.int32, (TOK, 128), 1)
    slot_s = lax.broadcasted_iota(jnp.int32, (TOK, 128), 0)
    laid = jnp.where(lane_s == lane0 + slot_s % SHARE, sent, 0.0).astype(BF16)
    by_group = (lax.broadcasted_iota(jnp.int32, (N_DP, TOK), 1) // SHARE
                == lax.broadcasted_iota(jnp.int32, (N_DP, TOK), 0)).astype(BF16)
    rows_out = jnp.dot(by_group, laid, preferred_element_type=F32)
    sub = lax.broadcasted_iota(jnp.int32, (N_DP, 8, 128), 1)
    lane3 = lax.broadcasted_iota(jnp.int32, (N_DP, 8, 128), 2)
    mine = (lane3 >= lane0) & (lane3 < lane0 + SHARE)
    len0 = jnp.minimum(len_ref[0], SLOT).astype(F32)
    len1 = jnp.minimum(len_ref[1], SLOT).astype(F32)
    possend[...] = jnp.where(sub == 0, rows_out.reshape(N_DP, 1, 128), jnp.where(
        mine, jnp.where(sub == 1, len0, jnp.where(sub == 2, len1, 0.0)), 0.0))

    def pos_msg(i):
        d = (dp + i) % N_DP
        return rcopy(possend.at[d], posbuf.at[dp], pos_s.at[0], pos_r.at[0], d, v)

    def cut(j):
        return pl.ds(j * CC, CC)

    def w_cols(xt, j):
        return pl.ds(pl.multiple_of(col_start(xt) + j * CC, 128), CC)

    def w_x(j, i):
        xt = (x + i) % 4
        return rcopy(w_hbm.at[:, w_cols(xt, j)], wbuf.at[dp, :, cut(j)], w_s.at[0], wx_r.at[j], y * 4 + xt, v)

    def y_to(i):
        return (y + i) % 4 * 4 + x

    def w_sem(j, k, i):
        if i == 1 and k in (0, 1):
            return wf_r.at[j, 0]
        if i == 3 and k in (2, 3):
            return wf_r.at[j, 1]
        return w_r.at[j]

    def w_own_y(j, i):
        return rcopy(w_hbm.at[:, w_cols(x, j)], wbuf.at[dp, :, cut(j)], w_s.at[0], w_sem(j, 0, i), y_to(i), v)

    def w_row_y(j, k, i):
        b = y * 4 + (x + k) % 4
        return rcopy(wbuf.at[b, :, cut(j)], wbuf.at[b, :, cut(j)], w_s.at[0], w_sem(j, k, i), y_to(i), v)

    def w_fwd(j, k, i):
        b = (y + 4 - i) % 4 * 4 + (x + k) % 4
        return rcopy(wbuf.at[b, :, cut(j)], wbuf.at[b, :, cut(j)], w_s.at[0], w_r.at[j], y_to(i), v)

    def w_arrived(j, n, sem):
        rcopy(wbuf.at[0:n, :, cut(j)], wbuf.at[0:n, :, cut(j)], w_s.at[0], sem, dp, v).wait_recv()

    pl.semaphore_wait(bar, 15 + 4 + 7)
    for i in range(1, N_DP):
        pos_msg(i).start()
    for j in range(NC):
        for i in (1, 3, 2):
            w_x(j, i).start()
        for i in (1, 3):
            w_own_y(j, i).start()
    posbuf[pl.ds(dp, 1)] = possend[pl.ds(dp, 1)]

    get_t.wait()

    def order(j, _):
        cols = pl.ds(pl.multiple_of(j * 256, 256), 256)
        res = jnp.dot(sel[...], tin[:, cols], preferred_element_type=F32).astype(BF16)
        tord[:, :, :, cols] = res.reshape(Q, 4, SHARE, 256)
        return 0

    lax.fori_loop(0, VSH // 256, order, 0)

    def t_msg(q, i):
        xt = (x + i) % 4
        return rcopy(tord.at[q, :, :, pl.ds(col_start(xt), CB)], tbuf.at[q, :, x], t_s.at[0], t_r.at[q], y * 4 + xt, v)

    t_own = pltpu.make_async_copy(tord.at[:, :, :, pl.ds(col_start(x), CB)], tbuf.at[:, :, x], lsem.at[1])
    t_own.start()

    def unit(vv):
        return vv % 4 * 4 + vv // 4

    rcopy(possend.at[0:15], posbuf.at[0:15], pos_s.at[0], pos_r.at[0], dp, v).wait_recv()
    low_t = jnp.sum(posbuf[0:8], axis=0)
    high_t = jnp.sum(posbuf[8:16], axis=0)
    seen = jnp.concatenate([low_t, high_t], axis=1)
    place = (lax.broadcasted_iota(jnp.int32, (TOK, TOK), 0).astype(F32) == seen[0:1, :]).astype(BF16)
    place_ref[...] = place
    get_h.wait()
    for j in range(5):
        hsend[:, j * 256:(j + 1) * 256] = lax.dot_general(
            place, hin[:, j * 256:(j + 1) * 256], (((0,), (0,)), ((), ())), preferred_element_type=F32).astype(BF16)

    def h_msg(i):
        d = (dp + i) % N_DP
        at = pl.ds(pl.multiple_of((d // 4 * 4 + v // 4) * SHARE, SHARE), SHARE)
        return rcopy(hsend.at[at], hbuf.at[y, unit(v)], hd_s.at[0], hd_r.at[y], d, v)

    @pl.when(x == v % 4)
    def _():
        for i in range(1, N_DP):
            h_msg(i).start()
        hbuf[pl.ds(y, 1), pl.ds(unit(v), 1)] = hsend[
            pl.ds(pl.multiple_of((y * 4 + v // 4) * SHARE, SHARE), SHARE)].reshape(1, 1, SHARE, FEAT)

    sent_row = jnp.broadcast_to(sent, (TOK, 128)).T[0:1, :]
    sent_in = jnp.where(sent_row >= SLOT, sent_row - SLOT, sent_row)
    valid = (sent_in < jnp.where(sent_row >= SLOT, seen[2:3, :], seen[1:2, :])).astype(F32)
    eighth = (lax.broadcasted_iota(jnp.int32, (8, TOK), 1) // 32
              == lax.broadcasted_iota(jnp.int32, (8, TOK), 0)).astype(F32)
    to_lane = (lane_s == slot_s // SHARE % 2 * 64 + x * SHARE + slot_s % SHARE).astype(BF16)
    valid8 = jnp.dot((eighth * valid).astype(BF16), to_lane, preferred_element_type=F32)
    valid8 = jnp.where(c == 0, valid8, 0.0)
    sub8 = lax.broadcasted_iota(jnp.int32, (8, 128), 0)
    for q in range(Q):
        vbuf[q] = jnp.where(sub8 == 3, valid8[2 * q:2 * q + 1, :], jnp.where(
            sub8 == 7, valid8[2 * q + 1:2 * q + 2, :], 0.0))
    count = jnp.sum(seen[1:3, :], keepdims=True) * (1.0 / SHARE)
    scale = float(TOK * N_DP) / count

    own_w.wait()

    def w_pass_x(j):
        w_arrived(j, 3, wx_r.at[j])
        for k in (1, 3, 2):
            for i in (1, 3):
                w_row_y(j, k, i).start()

    def w_pass_y(j):
        for way, (ks, i) in enumerate((((0, 1), 1), ((3, 2), 3))):
            w_arrived(j, 2, wf_r.at[j, way])
            for k in ks:
                w_fwd(j, k, i).start()

    def h_z(h, b, i, s):
        u = unit(b)
        at = hbuf.at[2 * h:2 * h + 2, u]
        return rcopy(at, at, h_s.at[0], hz_r.at[h, i // 4, s], dp, (z + i) % N_Z * 2 + c)

    def h_c(h, b):
        at = hbuf.at[2 * h:2 * h + 2, unit(b)]
        return rcopy(at, at, h_s.at[0], hc_r.at[0], dp, z * 2 + 1 - c)

    def h_first(h):
        for q in (2 * h, 2 * h + 1):
            @pl.when((x != v % 4) | (y != q))
            def _(q=q):
                rcopy(hsend.at[pl.ds(0, SHARE)], hbuf.at[q, unit(v)], hd_s.at[0], hd_r.at[q], dp, v).wait_recv()
        h_z(h, v, 1, 0).start()
        h_z(h, v, N_Z - 1, 0).start()
        h_c(h, v).start()

    def h_step(h, s):
        for way, i in ((0, 1), (1, N_Z - 1)):
            if s == 4 and way != h:
                continue
            b = (v + N_V + (2 * s if way else -2 * s)) % N_V
            h_z(h, b, i, s - 1).wait_recv()
            if s < 3 or (s == 3 and way == h):
                h_z(h, b, i, s).start()
            h_c(h, b).start()

    def t_send(q):
        for i in (1, 3, 2):
            t_msg(q, i).start()

    for j in range(NC):
        w_pass_x(j)
        if j == 2:
            t_send(0)
    for q in range(1, Q):
        t_send(q)
    h_first(0)
    h_first(1)
    w_pass_y(0)
    w_pass_y(1)
    h_step(0, 1)
    h_step(1, 1)
    w_pass_y(2)
    h_step(0, 2)
    h_step(1, 2)
    w_pass_y(3)
    w_pass_y(4)
    h_step(0, 3)
    h_step(1, 3)
    h_step(0, 4)
    h_step(1, 4)
    rcopy(hbuf.at[:, 0:8], hbuf.at[:, 0:8], h_s.at[0], hc_r.at[0], dp, v).wait_recv()

    odd = x % 2
    for j in range(NC):
        w_arrived(j, 8, w_r.at[j])

        def chunk(q, _, j=j):
            wj = wbuf[:, :, j * CC:(j + 1) * CC].reshape(FEAT, CC)
            out = jnp.dot(hbuf[pl.ds(q * 2, 2)].reshape(2 * TOK, FEAT), wj, preferred_element_type=F32)
            if j == 0:
                hidden = (lax.broadcasted_iota(jnp.int32, (2 * TOK, CC), 1) < 128) & (odd == 1)
                out = jnp.where(hidden, -BIG, out)
            lbuf[pl.ds(q * 2, 2), :, j * CC:(j + 1) * CC] = out.reshape(2, TOK, CC)
            return 0

        lax.fori_loop(0, 2, chunk, 0)

    lane_r = lax.broadcasted_iota(jnp.int32, (ROWS, 128), 1)
    me8 = x * 2 + c

    t_own.wait()

    def a_msg(q, i):
        k = (me8 + i) % 8
        return rcopy(asend.at[q], arecv.at[q, me8], a_s.at[0], a_r.at[q], y * 4 + k // 2, z * 2 + k % 2)

    def b_msg(q, i):
        return rcopy(bsend.at[q], brecv.at[q, z], b_s.at[0], b_r.at[q], dp, (z + i) % N_Z * 2 + c)

    def c_msg(q):
        return rcopy(part.at[q, :, 1 - c], corebuf.at[q], c_s.at[0], c_r.at[q], dp, z * 2 + 1 - c)

    def x_msg(q, i):
        xt = (x + i) % 4
        return rcopy(xs.at[q, xt], xr.at[q, x], x_s.at[0], x_r.at[q], y * 4 + xt, v)

    def z_msg(q, i):
        zt = (z + i) % N_Z
        return rcopy(zs.at[q, zt // 2], zr.at[q, z], z_s.at[0], z_r.at[q], dp, zt * 2 + c)

    def f_msg(q):
        return rcopy(fs.at[q], fr.at[y], f_s.at[0], f_r.at[0], q * 4 + x, v)

    def combine(got):
        halves = []
        for r in (0, 4):
            mxs = got[:, r:r + 1, :]
            mx = jnp.max(mxs, axis=0)
            ratio = jnp.exp(mxs - mx[None])
            halves.append((mx, jnp.sum(ratio * got[:, r + 1:r + 2, :], axis=0),
                           jnp.sum(ratio * got[:, r + 2:r + 3, :], axis=0)))
        return halves

    def stage0(q):
        rcopy(tbuf.at[q, :, 0:3], tbuf.at[q, :, 0:3], t_s.at[0], t_r.at[q], dp, v).wait_recv()

        def rows(r, _):
            at = pl.ds(pl.multiple_of(r * ROWS, ROWS), ROWS)
            logits = lbuf[q, at, :]
            targets = tbuf[q, r // 2, pl.ds(r % 2 * 2, 2)].reshape(ROWS, CB).astype(F32)
            mx = jnp.max(logits, axis=1, keepdims=True)
            e = jnp.exp(logits - mx)
            tot = jnp.sum(e, axis=1, keepdims=True)
            mom = jnp.sum(e * (logits - targets), axis=1, keepdims=True)
            base = r // 4 * 4
            statcol[at, :] = jnp.where(lane_r == base, mx, jnp.where(
                lane_r == base + 1, tot, jnp.where(lane_r == base + 2, mom, 0.0)))
            return 0

        lax.fori_loop(0, TOK // ROWS, rows, 0, unroll=4)
        packed = (statcol[0:128, :] + statcol[128:256, :]).T[0:8, :] + vbuf[q]
        asend[q] = packed
        for i in range(1, 8):
            a_msg(q, i).start()
        arecv[q, pl.ds(me8, 1)] = packed[None]

    def stage1(q):
        rcopy(arecv.at[q, 0:7], arecv.at[q, 0:7], a_s.at[0], a_r.at[q], dp, v).wait_recv()
        got = arecv[q]
        bits = jnp.sum(got, axis=0)
        (m0, t0, o0), (m1, t1, o1) = combine(got)
        packed = jnp.concatenate([m0, t0, o0, bits[3:4], m1, t1, o1, bits[7:8]], axis=0)
        bsend[q] = packed
        for i in range(1, N_Z):
            b_msg(q, i).start()
        brecv[q, pl.ds(z, 1)] = packed[None]

    def stage2(q):
        rcopy(brecv.at[q, 0:7], brecv.at[q, 0:7], b_s.at[0], b_r.at[q], dp, v).wait_recv()
        rows8 = []
        for half, (mx, tot, mom) in enumerate(combine(brecv[q])):
            weight = bsend[q, 4 * half + 3:4 * half + 4, :] * scale
            gap = mom / tot
            rows8 += [mx, weight / tot, gap, weight * (gap - mx - jnp.log(tot))]
        cols = jnp.concatenate(rows8 + [jnp.zeros((120, 128), F32)], axis=0).T
        ycol[...] = cols
        lane_f = lax.broadcasted_iota(jnp.int32, (128, 128), 1)
        for half in range(2):
            lossbuf[q, half * 128:(half + 1) * 128, :] = jnp.where(
                lane_f == FB, cols[:, 4 * half + 3:4 * half + 4], 0.0)

            def rows(r, _, half=half):
                yat = pl.ds(pl.multiple_of(r * ROWS, ROWS), ROWS)
                at = pl.ds(pl.multiple_of(half * 128 + r * ROWS, ROWS), ROWS)
                rr = half * 4 + r
                yc = ycol[yat, :]
                mx, inv, gap = (yc[:, 4 * half + k:4 * half + k + 1] for k in range(3))
                logits = lbuf[q, at, :]
                targets = tbuf[q, rr // 2, pl.ds(rr % 2 * 2, 2)].reshape(ROWS, CB).astype(F32)
                gbuf[at, :] = (jnp.exp(logits - mx) * inv * (logits - targets - gap)).astype(BF16)
                return 0

            lax.fori_loop(0, 4, rows, 0, unroll=4)

        out = lax.dot_general(
            wbuf[...].reshape(FEAT, CB), gbuf[...], (((1,), (1,)), ((), ())), preferred_element_type=F32)
        part[q] = out.reshape(N_Z, 2, FB, TOK)
        c_msg(q).start()

    low_lane = lax.broadcasted_iota(jnp.int32, (FB, 128), 1) < 64

    def stage3(q):
        c_msg(q).wait_recv()

        def pair(p, _):
            for h in range(2):
                even = part[q, 2 * p, c, :, h * 128:(h + 1) * 128] + corebuf[q, 2 * p, :, h * 128:(h + 1) * 128]
                odd_z = part[q, 2 * p + 1, c, :, h * 128:(h + 1) * 128] + corebuf[q, 2 * p + 1, :, h * 128:(h + 1) * 128]
                xs[q, 2 * h, p] = jnp.where(low_lane, even, pltpu.roll(odd_z, 64, 1)).astype(BF16)
                xs[q, 2 * h + 1, p] = jnp.where(low_lane, pltpu.roll(even, 64, 1), odd_z).astype(BF16)
            return 0

        lax.fori_loop(0, 4, pair, 0)
        for i in (1, 3, 2):
            x_msg(q, i).start()

    def stage4(q):
        total = xs[q, x].astype(F32)
        rcopy(xr.at[q, 0:3], xr.at[q, 0:3], x_s.at[0], x_r.at[q], dp, v).wait_recv()
        for i in (1, 3, 2):
            total += xr[q, (x + i) % 4].astype(F32)
        zs[q] = total.astype(BF16)
        for i in (1, 7, 2, 6, 3, 5, 4):
            z_msg(q, i).start()

    def stage5(q):
        total = zs[q, z // 2].astype(F32)
        rcopy(zr.at[q, 0:7], zr.at[q, 0:7], z_s.at[0], z_r.at[q], dp, v).wait_recv()
        for i in range(1, N_Z):
            total += zr[q, (z + i) % N_Z].astype(F32)
        tr[...] = jnp.concatenate([total, jnp.zeros((128 - FB, 128), F32)], axis=0).T
        mine_rows = tr[pl.ds(pl.multiple_of(z % 2 * 64, 64), 64), :] + lossbuf[q, pl.ds(pl.multiple_of(x * 64, 64), 64), :]
        fs[q] = mine_rows

        @pl.when(y == q)
        def _():
            fr[pl.ds(y, 1)] = mine_rows[None]

        @pl.when(y != q)
        def _():
            f_msg(q).start()

    stages = [stage0, stage1, stage2, stage3, stage4, stage5]

    def tick(tau, _):
        for s in (0, 1, 3, 4, 5, 2):
            q = tau - s

            @pl.when((q >= 0) & (q < Q))
            def _(s=s, q=q):
                stages[s](q)
        return 0

    lax.fori_loop(0, Q + len(stages) - 1, tick, 0)
    rcopy(fr.at[0:3], fr.at[0:3], f_s.at[0], f_r.at[0], dp, v).wait_recv()
    out_ref[...] = fr[...].reshape(TOK, 128)

    @pl.when(x == v % 4)
    def _():
        rcopy(hsend.at[0:15 * SHARE], hsend.at[0:15 * SHARE], hd_s.at[0], hd_r.at[0], dp, v).wait_send()

    for whole, ss, rs in (
        (wbuf.at[0:15], w_s, w_r), (posbuf.at[0:15], pos_s, pos_r), (hbuf.at[:, 0:15], h_s, hc_r),
        (tbuf.at[:, :, 0:3], t_s, t_r), (arecv.at[:, 0:7], a_s, a_r), (brecv.at[:, 0:7], b_s, b_r),
        (corebuf, c_s, c_r), (xr.at[:, 0:3], x_s, x_r), (zr.at[:, 0:7], z_s, z_r), (fr.at[0:3], f_s, f_r),
    ):
        rcopy(whole, whole, ss.at[0], rs.at[0], dp, v).wait_send()


def finish(rows_ref, place_ref, grad_ref, loss_ref):
    rows = rows_ref[...]
    hi = rows.astype(BF16)
    rest = rows - hi.astype(F32)
    mid = rest.astype(BF16)
    low = (rest - mid.astype(F32)).astype(BF16)
    placed = jnp.zeros((TOK, 128), F32)
    for piece in (low, mid, hi):
        placed += jnp.dot(place_ref[...], piece, preferred_element_type=F32)
    turned = placed.T
    grad_ref[...] = turned[0:FB, :]
    loss_ref[...] = turned[FB:FB + 1, :]


def per_device(hidden_states, head_weight, teacher_logprobs, teacher_dest, lengths):
    vm = pltpu.VMEM
    dma = pltpu.SemaphoreType.DMA
    rows, place = pl.pallas_call(
        kernel,
        out_shape=(jax.ShapeDtypeStruct((TOK, 128), F32), jax.ShapeDtypeStruct((TOK, TOK), BF16)),
        in_specs=[pl.BlockSpec(memory_space=pltpu.VMEM), pl.BlockSpec(memory_space=pltpu.SMEM)]
        + [pl.BlockSpec(memory_space=pl.ANY)] * 3,
        out_specs=(pl.BlockSpec(memory_space=pltpu.VMEM), pl.BlockSpec(memory_space=pltpu.VMEM)),
        scratch_shapes=[
            vm((TOK, VSH), BF16),
            vm((TOK, FEAT), BF16),
            vm((N_DP, FB, CB), BF16),
            vm((Q, 4, SHARE, VSH), BF16),
            vm((Q, 4, 4, SHARE, CB), BF16),
            vm((TOK, FEAT), BF16),
            vm((Q, N_DP, SHARE, FEAT), BF16),
            vm((N_DP, 8, 128), F32),
            vm((N_DP, 8, 128), F32),
            vm((TOK, TOK), BF16),
            vm((Q, 8, 128), F32),
            vm((Q, TOK, CB), F32),
            vm((TOK, CB), BF16),
            vm((TOK, 128), F32),
            vm((128, 128), F32),
            vm((Q, TOK, 128), F32),
            vm((Q, 8, 128), F32),
            vm((Q, 8, 8, 128), F32),
            vm((Q, 8, 128), F32),
            vm((Q, N_Z, 8, 128), F32),
            vm((Q, N_Z, 2, FB, TOK), F32),
            vm((Q, N_Z, FB, TOK), F32),
            vm((Q, 4, 4, FB, 128), BF16),
            vm((Q, 4, 4, FB, 128), BF16),
            vm((Q, 4, FB, 128), BF16),
            vm((Q, N_Z, FB, 128), BF16),
            vm((128, 128), F32),
            vm((Q, 64, 128), F32),
            vm((4, 64, 128), F32),
            dma((3,)),
            dma((1,)), dma((NC,)), dma((NC, 2)), dma((NC,)),
            dma((1,)), dma((1,)),
            dma((1,)), dma((Q,)),
            dma((1,)), dma((2, 2, 4)), dma((1,)),
            dma((1,)), dma((Q,)),
            dma((1,)), dma((Q,)),
            dma((1,)), dma((Q,)),
            dma((1,)), dma((Q,)),
            dma((1,)), dma((Q,)),
            dma((1,)), dma((Q,)),
            dma((1,)), dma((Q,)),
        ],
        compiler_params=pltpu.CompilerParams(
            collective_id=0, has_side_effects=True, vmem_limit_bytes=58 * 2**20),
        name="distill",
    )(teacher_dest.reshape(2, 128), lengths, hidden_states, head_weight, teacher_logprobs)
    grad, loss = pl.pallas_call(
        finish,
        out_shape=(jax.ShapeDtypeStruct((FB, TOK), F32), jax.ShapeDtypeStruct((1, TOK), F32)),
        name="finish",
    )(rows, place)
    return grad.T, loss.reshape(TOK)


def solution(mesh):
    placed = (P("dp", None), P("dp", "vocab"), P("dp", "vocab"), P("dp"), P("dp"))
    return jax.shard_map(
        per_device,
        mesh=mesh,
        in_specs=placed,
        out_specs=(P("dp", "vocab"), P("dp")),
        check_vma=False,
    )
```

time: 144 us -> 103 us (0.72)
  Pallas kernels: 140 us -> 102 us
  local copies, waits for them, and re-layouts: 2.85 us -> 0 us
    pallas_call x1 -> x2, Pallas kernels: 140 us -> 102 us  [the longest x1 100 us: per_device(): pl.pallas_call(kernel, out_shape=(jax.ShapeDtypeStruct((TOK, 128), F32),...]
    unnamed x2 -> x0, local copies, waits for them, and re-layouts: 2.85 us -> none
where the time goes in v2:
time: 103 us
  Pallas kernels  102 us (99%)
    pallas_call x1, Pallas kernels, per_device(): pl.pallas_call(kernel, out_shape=(jax.ShapeDtypeStruct((TOK, 128), F32),...  100 us

profile of v2, /device:TPU:24, one launch (start us, length us, event | category | flops | bytes accessed | tf_op | source)
XLA Modules:
  0.0 102.7 jit_solution(14486390465234770172)
XLA Ops:
  0.6 100.1 %distill.1 = (f32[256,128]{1,0:T(8,128)}, bf16[256,256]{1,0:T(8,128)(2,1)}) custom-call(s32[2,128]{1,0:T(2,128)} %bitcast.3, s32[2]{0:T(128)} %len_ref.1, bf16[256,1280]{1,0:T(8,128)(2,1)} %h_hbm.1, bf16[80,4864]{1,0:T(8,128)(2,1)} %w_hbm.1, bf16[256,4864]{1,0:T(8,128)(2,1)} %t_hbm.1), custom_call_target="tpu_custom_call" | custom-call | tf_op jit(solution)/shard_map/distill/pallas_call | solution.py:475
  100.8 1.9 %finish.1 = (f32[80,256]{1,0:T(8,128)}, f32[1,256]{1,0:T(1,128)}) custom-call(f32[256,128]{1,0:T(8,128)} %get-tuple-element.6.rows_ref, bf16[256,256]{1,0:T(8,128)(2,1)} %get-tuple-element.7.place_ref), custom_call_target="tpu_custom_call" | custom-call | tf_op jit(solution)/shard_map/finish/pallas_call | solution.py:528

commit v3 on v2

--- a/solution.py
+++ b/solution.py
@@ -22,6 +22,8 @@
 Q = 4
 ROWS = 32
 BIG = 1e30
+OFFSET = (0, 1, 3, 4, 6, 8)
+ZQ = 0
 F32, BF16 = jnp.float32, jnp.bfloat16
 
 
@@ -141,26 +143,24 @@
             w_own_y(j, i).start()
     posbuf[pl.ds(dp, 1)] = possend[pl.ds(dp, 1)]
 
-    get_t.wait()
-
-    def order(j, _):
-        cols = pl.ds(pl.multiple_of(j * 256, 256), 256)
-        res = jnp.dot(sel[...], tin[:, cols], preferred_element_type=F32).astype(BF16)
-        tord[:, :, :, cols] = res.reshape(Q, 4, SHARE, 256)
-        return 0
-
-    lax.fori_loop(0, VSH // 256, order, 0)
-
-    def t_msg(q, i):
-        xt = (x + i) % 4
-        return rcopy(tord.at[q, :, :, pl.ds(col_start(xt), CB)], tbuf.at[q, :, x], t_s.at[0], t_r.at[q], y * 4 + xt, v)
-
-    t_own = pltpu.make_async_copy(tord.at[:, :, :, pl.ds(col_start(x), CB)], tbuf.at[:, :, x], lsem.at[1])
-    t_own.start()
-
     def unit(vv):
         return vv % 4 * 4 + vv // 4
 
+    own_w.wait()
+
+    def w_pass_x(j):
+        w_arrived(j, 3, wx_r.at[j])
+        for k in (1, 3, 2):
+            for i in (1, 3):
+                w_row_y(j, k, i).start()
+
+    def w_pass_y(j):
+        for way, (ks, i) in enumerate((((0, 1), 1), ((3, 2), 3))):
+            w_arrived(j, 2, wf_r.at[j, way])
+            for k in ks:
+                w_fwd(j, k, i).start()
+
+    w_pass_x(0)
     rcopy(possend.at[0:15], posbuf.at[0:15], pos_s.at[0], pos_r.at[0], dp, v).wait_recv()
     low_t = jnp.sum(posbuf[0:8], axis=0)
     high_t = jnp.sum(posbuf[8:16], axis=0)
@@ -183,6 +183,25 @@
             h_msg(i).start()
         hbuf[pl.ds(y, 1), pl.ds(unit(v), 1)] = hsend[
             pl.ds(pl.multiple_of((y * 4 + v // 4) * SHARE, SHARE), SHARE)].reshape(1, 1, SHARE, FEAT)
+
+    w_pass_x(1)
+    get_t.wait()
+
+    def order(j, _):
+        cols = pl.ds(pl.multiple_of(j * 256, 256), 256)
+        res = jnp.dot(sel[...], tin[:, cols], preferred_element_type=F32).astype(BF16)
+        tord[:, :, :, cols] = res.reshape(Q, 4, SHARE, 256)
+        return 0
+
+    lax.fori_loop(0, VSH // 256, order, 0)
+
+    def t_msg(q, i):
+        xt = (x + i) % 4
+        return rcopy(tord.at[q, :, :, pl.ds(col_start(xt), CB)], tbuf.at[q, :, x], t_s.at[0], t_r.at[q], y * 4 + xt, v)
+
+    t_own = pltpu.make_async_copy(tord.at[:, :, :, pl.ds(col_start(x), CB)], tbuf.at[:, :, x], lsem.at[1])
+    t_own.start()
+    w_pass_x(2)
 
     sent_row = jnp.broadcast_to(sent, (TOK, 128)).T[0:1, :]
     sent_in = jnp.where(sent_row >= SLOT, sent_row - SLOT, sent_row)
@@ -199,89 +218,80 @@
     count = jnp.sum(seen[1:3, :], keepdims=True) * (1.0 / SHARE)
     scale = float(TOK * N_DP) / count
 
-    own_w.wait()
-
-    def w_pass_x(j):
-        w_arrived(j, 3, wx_r.at[j])
-        for k in (1, 3, 2):
-            for i in (1, 3):
-                w_row_y(j, k, i).start()
-
-    def w_pass_y(j):
-        for way, (ks, i) in enumerate((((0, 1), 1), ((3, 2), 3))):
-            w_arrived(j, 2, wf_r.at[j, way])
-            for k in ks:
-                w_fwd(j, k, i).start()
-
-    def h_z(h, b, i, s):
-        u = unit(b)
-        at = hbuf.at[2 * h:2 * h + 2, u]
-        return rcopy(at, at, h_s.at[0], hz_r.at[h, i // 4, s], dp, (z + i) % N_Z * 2 + c)
-
-    def h_c(h, b):
-        at = hbuf.at[2 * h:2 * h + 2, unit(b)]
+    def h_z(q, b, i, s):
+        at = hbuf.at[q, unit(b)]
+        return rcopy(at, at, h_s.at[0], hz_r.at[q, i // 4, s], dp, (z + i) % N_Z * 2 + c)
+
+    def h_c(q, b):
+        at = hbuf.at[q, unit(b)]
         return rcopy(at, at, h_s.at[0], hc_r.at[0], dp, z * 2 + 1 - c)
 
-    def h_first(h):
-        for q in (2 * h, 2 * h + 1):
-            @pl.when((x != v % 4) | (y != q))
-            def _(q=q):
-                rcopy(hsend.at[pl.ds(0, SHARE)], hbuf.at[q, unit(v)], hd_s.at[0], hd_r.at[q], dp, v).wait_recv()
-        h_z(h, v, 1, 0).start()
-        h_z(h, v, N_Z - 1, 0).start()
-        h_c(h, v).start()
-
-    def h_step(h, s):
-        for way, i in ((0, 1), (1, N_Z - 1)):
-            if s == 4 and way != h:
-                continue
-            b = (v + N_V + (2 * s if way else -2 * s)) % N_V
-            h_z(h, b, i, s - 1).wait_recv()
-            if s < 3 or (s == 3 and way == h):
-                h_z(h, b, i, s).start()
-            h_c(h, b).start()
+    def h_first(q):
+        @pl.when((x != v % 4) | (y != q))
+        def _():
+            rcopy(hsend.at[pl.ds(0, SHARE)], hbuf.at[q, unit(v)], hd_s.at[0], hd_r.at[q], dp, v).wait_recv()
+        h_z(q, v, 1, 0).start()
+        h_z(q, v, N_Z - 1, 0).start()
+        h_c(q, v).start()
+
+    def h_steps(s):
+        def step(q, _):
+            for way, i in ((0, 1), (1, N_Z - 1)):
+                def piece(way=way, i=i):
+                    b = (v + N_V + (2 * s if way else -2 * s)) % N_V
+                    h_z(q, b, i, s - 1).wait_recv()
+                    if s < 3:
+                        h_z(q, b, i, s).start()
+                    elif s == 3:
+                        pl.when(q % 2 == way)(lambda: h_z(q, b, i, s).start())
+                    h_c(q, b).start()
+
+                if s < 4:
+                    piece()
+                else:
+                    pl.when(q % 2 == way)(piece)
+            return 0
+
+        lax.fori_loop(0, Q, step, 0)
 
     def t_send(q):
         for i in (1, 3, 2):
             t_msg(q, i).start()
 
-    for j in range(NC):
-        w_pass_x(j)
-        if j == 2:
-            t_send(0)
-    for q in range(1, Q):
-        t_send(q)
-    h_first(0)
-    h_first(1)
+    t_send(0)
+    w_pass_x(3)
+    w_pass_x(4)
+    t_send(1)
+    for q in range(Q):
+        h_first(q)
     w_pass_y(0)
+    h_steps(1)
     w_pass_y(1)
-    h_step(0, 1)
-    h_step(1, 1)
     w_pass_y(2)
-    h_step(0, 2)
-    h_step(1, 2)
+    h_steps(2)
+    t_send(2)
     w_pass_y(3)
+    h_steps(3)
     w_pass_y(4)
-    h_step(0, 3)
-    h_step(1, 3)
-    h_step(0, 4)
-    h_step(1, 4)
+    h_steps(4)
+    t_send(3)
     rcopy(hbuf.at[:, 0:8], hbuf.at[:, 0:8], h_s.at[0], hc_r.at[0], dp, v).wait_recv()
 
     odd = x % 2
-    for j in range(NC):
-        w_arrived(j, 8, w_r.at[j])
-
-        def chunk(q, _, j=j):
-            wj = wbuf[:, :, j * CC:(j + 1) * CC].reshape(FEAT, CC)
-            out = jnp.dot(hbuf[pl.ds(q * 2, 2)].reshape(2 * TOK, FEAT), wj, preferred_element_type=F32)
-            if j == 0:
-                hidden = (lax.broadcasted_iota(jnp.int32, (2 * TOK, CC), 1) < 128) & (odd == 1)
-                out = jnp.where(hidden, -BIG, out)
-            lbuf[pl.ds(q * 2, 2), :, j * CC:(j + 1) * CC] = out.reshape(2, TOK, CC)
+    def logit_chunk(j, _):
+        at = pl.ds(pl.multiple_of(j * CC, CC), CC)
+        rcopy(wbuf.at[0:8, :, at], wbuf.at[0:8, :, at], w_s.at[0], w_r.at[j], dp, v).wait_recv()
+        hidden = (lax.broadcasted_iota(jnp.int32, (2 * TOK, CC), 1) < 128) & (odd == 1) & (j == 0)
+
+        def half(h, _):
+            out = jnp.dot(hbuf[pl.ds(h * 2, 2)].reshape(2 * TOK, FEAT), wbuf[:, :, at].reshape(FEAT, CC),
+                          preferred_element_type=F32)
+            lbuf[pl.ds(h * 2, 2), :, at] = jnp.where(hidden, -BIG, out).reshape(2, TOK, CC)
             return 0
 
-        lax.fori_loop(0, 2, chunk, 0)
+        return lax.fori_loop(0, 2, half, 0)
+
+    lax.fori_loop(0, NC, logit_chunk, 0)
 
     lane_r = lax.broadcasted_iota(jnp.int32, (ROWS, 128), 1)
     me8 = x * 2 + c
@@ -387,6 +397,19 @@
 
     low_lane = lax.broadcasted_iota(jnp.int32, (FB, 128), 1) < 64
 
+    def deliver(q, total, half):
+        tr[...] = jnp.concatenate([total, jnp.zeros((128 - FB, 128), F32)], axis=0).T
+        mine_rows = tr[pl.ds(pl.multiple_of(half * 64, 64), 64), :] + lossbuf[q, pl.ds(pl.multiple_of(x * 64, 64), 64), :]
+        fs[q] = mine_rows
+
+        @pl.when(y == q)
+        def _():
+            fr[pl.ds(y, 1)] = mine_rows[None]
+
+        @pl.when(y != q)
+        def _():
+            f_msg(q).start()
+
     def stage3(q):
         c_msg(q).wait_recv()
 
@@ -416,30 +439,25 @@
         rcopy(zr.at[q, 0:7], zr.at[q, 0:7], z_s.at[0], z_r.at[q], dp, v).wait_recv()
         for i in range(1, N_Z):
             total += zr[q, (z + i) % N_Z].astype(F32)
-        tr[...] = jnp.concatenate([total, jnp.zeros((128 - FB, 128), F32)], axis=0).T
-        mine_rows = tr[pl.ds(pl.multiple_of(z % 2 * 64, 64), 64), :] + lossbuf[q, pl.ds(pl.multiple_of(x * 64, 64), 64), :]
-        fs[q] = mine_rows
-
-        @pl.when(y == q)
-        def _():
-            fr[pl.ds(y, 1)] = mine_rows[None]
-
-        @pl.when(y != q)
-        def _():
-            f_msg(q).start()
-
-    stages = [stage0, stage1, stage2, stage3, stage4, stage5]
+        deliver(q, total, z % 2)
+
+    stages = (stage0, stage1, stage2, stage3, stage4, stage5)
+    stages_z = {}
 
     def tick(tau, _):
-        for s in (0, 1, 3, 4, 5, 2):
-            q = tau - s
-
-            @pl.when((q >= 0) & (q < Q))
+        for s in (0, 1, 2, 3, 4, 5):
+            q = tau - OFFSET[s]
+            if s in stages_z and ZQ:
+                @pl.when((q >= 0) & (q < ZQ))
+                def _(s=s, q=q):
+                    stages_z[s](q)
+
+            @pl.when((q >= (ZQ if s in stages_z else 0)) & (q < Q))
             def _(s=s, q=q):
                 stages[s](q)
         return 0
 
-    lax.fori_loop(0, Q + len(stages) - 1, tick, 0)
+    lax.fori_loop(0, Q + OFFSET[-1], tick, 0)
     rcopy(fr.at[0:3], fr.at[0:3], f_s.at[0], f_r.at[0], dp, v).wait_recv()
     out_ref[...] = fr[...].reshape(TOK, 128)
 
@@ -450,7 +468,7 @@
     for whole, ss, rs in (
         (wbuf.at[0:15], w_s, w_r), (posbuf.at[0:15], pos_s, pos_r), (hbuf.at[:, 0:15], h_s, hc_r),
         (tbuf.at[:, :, 0:3], t_s, t_r), (arecv.at[:, 0:7], a_s, a_r), (brecv.at[:, 0:7], b_s, b_r),
-        (corebuf, c_s, c_r), (xr.at[:, 0:3], x_s, x_r), (zr.at[:, 0:7], z_s, z_r), (fr.at[0:3], f_s, f_r),
+        (corebuf, c_s, c_r), (xr.at[ZQ:, 0:3], x_s, x_r), (zr.at[ZQ:, 0:7], z_s, z_r), (fr.at[0:3], f_s, f_r),
     ):
         rcopy(whole, whole, ss.at[0], rs.at[0], dp, v).wait_send()
 
@@ -512,7 +530,7 @@
             dma((1,)), dma((NC,)), dma((NC, 2)), dma((NC,)),
             dma((1,)), dma((1,)),
             dma((1,)), dma((Q,)),
-            dma((1,)), dma((2, 2, 4)), dma((1,)),
+            dma((1,)), dma((Q, 2, 4)), dma((1,)),
             dma((1,)), dma((Q,)),
             dma((1,)), dma((Q,)),
             dma((1,)), dma((Q,)),

time: 103 us -> 94 us (0.913)
  Pallas kernels: 102 us -> 93.3 us
    pallas_call x1, Pallas kernels: 100 us -> 91.3 us  [per_device(): pl.pallas_call(kernel, out_shape=(jax.ShapeDtypeStruct((TOK, 128), F32),...]
where the time goes in v3:
time: 94 us; the launch traced here: 93.9 us
  Pallas kernels  93.3 us (99%)
    pallas_call x1, Pallas kernels, per_device(): pl.pallas_call(kernel, out_shape=(jax.ShapeDtypeStruct((TOK, 128), F32),...  91.3 us
    pallas_call x1, Pallas kernels, per_device(): pl.pallas_call(finish, out_shape=(jax.ShapeDtypeStruct((FB, TOK), F32), j...  1.91 us

profile of v3, /device:TPU:24, one launch (start us, length us, event | category | flops | bytes accessed | tf_op | source)
XLA Modules:
  0.0 93.9 jit_solution(9389478434370045645)
XLA Ops:
  0.6 91.3 %distill.1 = (f32[256,128]{1,0:T(8,128)}, bf16[256,256]{1,0:T(8,128)(2,1)}) custom-call(s32[2,128]{1,0:T(2,128)} %bitcast.3, s32[2]{0:T(128)} %len_ref.1, bf16[256,1280]{1,0:T(8,128)(2,1)} %h_hbm.1, bf16[80,4864]{1,0:T(8,128)(2,1)} %w_hbm.1, bf16[256,4864]{1,0:T(8,128)(2,1)} %t_hbm.1), custom_call_target="tpu_custom_call" | custom-call | tf_op jit(solution)/shard_map/distill/pallas_call | solution.py:493
  92.0 1.9 %finish.1 = (f32[80,256]{1,0:T(8,128)}, f32[1,256]{1,0:T(1,128)}) custom-call(f32[256,128]{1,0:T(8,128)} %get-tuple-element.6.rows_ref, bf16[256,256]{1,0:T(8,128)(2,1)} %get-tuple-element.7.place_ref), custom_call_target="tpu_custom_call" | custom-call | tf_op jit(solution)/shard_map/finish/pallas_call | solution.py:546
